TPU v7x, 256 devices: a whole 4x4x8 slice. The times are simulated.
256 devices in a mesh: dp: 16 (over z, core), prec: 16 (over x, y).
Axes of the slice: x: 4, y: 4, z: 8, core: 2. Of those that a mesh axis runs over, the one named last changes fastest.
Arguments:
- activations: bfloat16 [4096, 8192], P('dp'), may hold values from -6 to 6
- cotangents: bfloat16 [4096, 8192], P('dp', 'prec'), may hold values from -0.09375 to 0.09375
- owner_slots: int32 [16, 16], P('dp'), may hold values from 0 to 31, as said below
- left_stats: float32 [16, 32, 512, 512], P('dp', 'prec'), as said below
- right_stats: float32 [16, 32, 512, 512], P('dp', 'prec'), as said below
Outputs:
- precond_update: bfloat16 [8192, 8192], P('dp', 'prec')
- left_fresh: float32 [16, 32, 512, 512], P('dp', 'prec')
- right_fresh: float32 [16, 32, 512, 512], P('dp', 'prec')
Inputs may be any that keep to these rules, and one draw needn't show every extreme that they name: `owner_slots`: in each row the 16 blocks name distinct slots; slot q belongs to owner q // 2; an owner holds at most 2 blocks of a row and its blocks occupy its lowest slots; in every row some owner holds exactly 2. `left_stats`: every slot holds a symmetric positive definite matrix. `right_stats`: every slot holds a symmetric positive definite matrix.
All inputs are finite; a program needn't handle non-finite values. Where the computation divides by a largest or mean magnitude, that divisor is 1e-20 or more.
Results may differ from a plain program's by a relative error of at most 0.027.
Values may be sent and summed in bfloat16 or wider, within the bound.
A program may use at most 128 MiB of HBM per device.

v0:
```python
import jax
import jax.numpy as jnp
from jax import lax
from jax.sharding import PartitionSpec as P

ITERS = 3
CAP = 2


decay_rate = 0.95


def matmul_bf(left_op, right_op):
    return jnp.dot(
        left_op.astype(jnp.bfloat16),
        right_op.astype(jnp.bfloat16),
        preferred_element_type=jnp.float32,
    )


def inverse_root(matrix):
    blk_size = matrix.shape[0]
    ident_mat = jnp.eye(blk_size, dtype=jnp.float32)
    row_sum = jnp.max(jnp.sum(jnp.abs(matrix), axis=1)) + 1e-06
    z_scale = 2.5 / row_sum
    moment = z_scale * matrix
    factor = (5.0 * ident_mat - moment) * 0.25
    result = jnp.sqrt(jnp.sqrt(z_scale)) * factor
    for rounds in range(1, ITERS):
        square = matmul_bf(factor, factor)
        moment = matmul_bf(square, matmul_bf(square, moment))
        factor = (5.0 * ident_mat - moment) * 0.25
        result = matmul_bf(result, factor)
    return result


def block_step(grad_block, left_old, right_old):
    blk_size = grad_block.shape[0]
    left_gram = lax.dot_general(
        grad_block, grad_block, (((1,), (1,)), ((), ())), preferred_element_type=jnp.float32
    )
    right_gram = lax.dot_general(
        grad_block, grad_block, (((0,), (0,)), ((), ())), preferred_element_type=jnp.float32
    )
    left_new = decay_rate * left_old + left_gram / blk_size
    right_new = decay_rate * right_old + right_gram / blk_size
    left_root = inverse_root(left_new)
    right_root = inverse_root(right_new)
    halfway = jnp.dot(
        grad_block, right_root.astype(jnp.bfloat16), preferred_element_type=jnp.float32
    ).astype(jnp.bfloat16)
    update = jnp.dot(
        left_root.astype(jnp.bfloat16), halfway, preferred_element_type=jnp.float32
    ).astype(jnp.bfloat16)
    return (left_new, right_new, update)


def shards(activations, cotangents, owner_slots, left_stats, right_stats):
    n_prec = lax.axis_size("prec")
    my_owner = lax.axis_index("prec")
    blk_size = cotangents.shape[1]
    slab_rows = blk_size // n_prec
    gradient = lax.psum_scatter(
        lax.dot_general(
            activations, cotangents, (((0,), (0,)), ((), ())), preferred_element_type=jnp.float32
        ).astype(jnp.bfloat16),
        "dp",
        scatter_dimension=0,
        tiled=True,
    )
    slot_row = owner_slots[0]
    slot_ids = jnp.arange(n_prec * CAP, dtype=jnp.int32)
    matches = slot_row[None, :] == slot_ids[:, None]
    filled = jnp.any(matches, axis=1)
    block_of = jnp.sum(jnp.where(matches, jnp.arange(n_prec, dtype=jnp.int32)[None, :], 0), axis=1)
    own_filled = lax.dynamic_slice_in_dim(filled, my_owner * CAP, CAP)
    back_idx = slot_row % CAP * n_prec + slot_row // CAP
    left_own = left_stats[0]
    right_own = right_stats[0]
    pieces = gradient.reshape(n_prec, slab_rows, blk_size)
    slab_parts = lax.all_to_all(pieces, "prec", split_axis=0, concat_axis=0, tiled=True)
    order_idx = block_of.reshape(n_prec, CAP).T.reshape(-1)
    fill_mask = filled.reshape(n_prec, CAP).T.reshape(-1)
    outgoing = jnp.where(
        fill_mask[:, None, None],
        jnp.take(slab_parts, order_idx, axis=0),
        jnp.zeros((), jnp.bfloat16),
    )
    outgoing = outgoing.reshape(CAP, n_prec, slab_rows, blk_size)
    arrived = lax.all_to_all(outgoing, "prec", split_axis=1, concat_axis=2, tiled=True).reshape(
        CAP, blk_size, blk_size
    )
    held_count = jnp.sum(own_filled.astype(jnp.int32))

    def per_slot(slot_pos, state_acc):
        left_acc, right_acc, upd_acc = state_acc
        left_one, right_one, upd_one = block_step(
            arrived[slot_pos], left_acc[slot_pos], right_acc[slot_pos]
        )
        return (
            left_acc.at[slot_pos].set(left_one),
            right_acc.at[slot_pos].set(right_one),
            upd_acc.at[slot_pos].set(upd_one),
        )

    left_out, right_out, upd_slots = lax.fori_loop(
        0,
        held_count,
        per_slot,
        (left_own, right_own, jnp.zeros((CAP, blk_size, blk_size), jnp.bfloat16)),
    )
    sending = upd_slots.reshape(CAP, n_prec, slab_rows, blk_size)
    pieces_back = lax.all_to_all(sending, "prec", split_axis=1, concat_axis=1, tiled=True)
    flat_back = pieces_back.reshape(CAP * n_prec, slab_rows, blk_size)
    per_block = jnp.take(flat_back, back_idx, axis=0)
    home_rows = lax.all_to_all(per_block, "prec", split_axis=0, concat_axis=1, tiled=True)
    update = home_rows.reshape(blk_size, blk_size)
    return (update, left_out[None], right_out[None])


def solution(mesh):
    placed = (
        P("dp", None),
        P("dp", "prec"),
        P("dp", None),
        P("dp", "prec", None, None),
        P("dp", "prec", None, None),
    )
    return jax.shard_map(
        shards,
        mesh=mesh,
        in_specs=placed,
        out_specs=(P("dp", "prec"), P("dp", "prec", None, None), P("dp", "prec", None, None)),
        check_vma=False,
    )
```

profile of v0, /device:TPU:64, one launch (start us, length us, event | category | flops | bytes accessed | tf_op | source)
XLA Modules:
  0.0 259.8 jit_solution(12673237341091131106)
XLA Ops:
  8.1 7.8 %convolution_convert_fusion.14 = bf16[8192,512]{1,0:T(8,128)(2,1)} fusion(bf16[256,8192]{1,0:T(8,128)(2,1)} %param.13, bf16[256,512]{1,0:T(8,128)(2,1)S(1)} %copy-done), kind=kOutput, calls=%fused_computation.101 | convolution fusion | flops 2151677952 | bytes 12845056 | tf_op jit(solution)/shard_map/dot_general | solution.py:64
  16.7 66.1 %reduce-scatter.2.cloned.1.call-done = bf16[512,512]{1,0:T(8,128)(2,1)} async-done(((bf16[8192,512]{1,0:T(8,128)(2,1)}), bf16[512,512]{1,0:T(8,128)(2,1)}) %reduce-scatter.2.cloned.1.call-update) | async-done | bytes 524304 | tf_op jit(solution)/shard_map/reduce_scatter | solution.py:63
  82.8 6.8 %all-to-all-start = ((bf16[16,32,512]{2,1,0:T(8,128)(2,1)}), bf16[16,32,512]{2,1,0:T(8,128)(2,1)S(1)}, u32[]{:S(2)}, u32[]{:S(2)}) async-start(bf16[16,32,512]{2,1,0:T(8,128)(2,1)} %bitcast.120), calls=%async_computation.1 | async-start | bytes 1048576 | tf_op jit(solution)/shard_map/all_to_all | solution.py:81
  90.2 9.5 %all-to-all-done = bf16[16,32,512]{2,1,0:T(8,128)(2,1)S(1)} async-done(((bf16[16,32,512]{2,1,0:T(8,128)(2,1)}), bf16[16,32,512]{2,1,0:T(8,128)(2,1)S(1)}, u32[]{:S(2)}, u32[]{:S(2)}) %all-to-all-start) | async-done | bytes 524320 | tf_op jit(solution)/shard_map/all_to_all | solution.py:81
  101.5 4.2 %all-to-all-start.1 = ((bf16[2,16,32,512]{3,2,0,1:T(8,128)(2,1)}), bf16[2,16,32,512]{3,2,0,1:T(8,128)(2,1)S(1)}, u32[]{:S(2)}, u32[]{:S(2)}) async-start(bf16[2,16,32,512]{3,2,0,1:T(8,128)(2,1)} %copy.69), calls=%async_computation.2 | async-start | bytes 2097152 | tf_op jit(solution)/shard_map/all_to_all | solution.py:90
  108.3 2.9 %copy.65 = f32[1,2,512,512]{2,3,1,0:T(8,128)} copy(f32[1,2,512,512]{3,2,1,0:T(8,128)} %param.17) | data formatting | bytes 4194304 | tf_op args[4]
  111.2 10.7 %all-to-all-done.1 = bf16[2,16,32,512]{3,2,0,1:T(8,128)(2,1)S(1)} async-done(((bf16[2,16,32,512]{3,2,0,1:T(8,128)(2,1)}), bf16[2,16,32,512]{3,2,0,1:T(8,128)(2,1)S(1)}, u32[]{:S(2)}, u32[]{:S(2)}) %all-to-all-start.1) | async-done | bytes 1048608 | tf_op jit(solution)/shard_map/all_to_all | solution.py:90
  124.0 83.1 %while.17 = (s32[]{:T(128)}, f32[2,512,512]{1,2,0:T(8,128)}, f32[2,512,512]{1,2,0:T(8,128)}, bf16[2,512,512]{2,1,0:T(8,128)(2,1)}, s32[]{:T(128)}, /*index=5*/bf...) while((s32[]{:T(128)}, f32[2,512,512]{1,2,0:T(8,128)}, ...), condition=%wide.region_10.11_spmd, body=%wide.region_4.10_spmd.sunk | while | flops 5391515648 | bytes 44577632 | solution.py:106
  124.8 2.1 abs_reduce_fusion.4
  131.2 2.9 %fusion.160 = bf16[512,512]{0,1:T(8,128)(2,1)} fusion(bf16[512,512]{1,0:T(8,128)(2,1)} %convolution_convert_fusion.25, f32[512,512]{1,0:T(8,128)S(1)} %fusion.159), kind=kOutput, calls=%fused_computation.29.clone.1 | convolution fusion | flops 538705920 | bytes 2097152 | tf_op jit(solution)/shard_map/while/body/dot_general | solution.py:14
  134.2 2.6 %convolution_convert_fusion.26 = bf16[512,512]{1,0:T(8,128)(2,1)} fusion(bf16[512,512]{0,1:T(8,128)(2,1)} %fusion.160, f32[512,512]{0,1:T(8,128)S(1)} %get-tuple-element.139, f32[]{:T(128)S(6)} %mul.309, f32[]{:T(128)S(6)} %div.79, f32[512,512]{0,1:T(8,128)S(1)} %copy.88), kind=kOutput, calls=%fused_computation.16.clone.1 | convolution fusion | flops 540278784 | bytes 3145736 | tf_op jit(solution)/shard_map/while/body/dot_general | solution.py:14
  141.5 2.1 fusion.157
  145.0 2.8 %convolution_convert_fusion.22 = bf16[512,512]{1,0:T(8,128)(2,1)} fusion(f32[512,512]{0,1:T(8,128)} %copy.87), kind=kOutput, calls=%fused_computation.24.clone.1 | convolution fusion | flops 270008320 | bytes 1572864 | tf_op jit(solution)/shard_map/while/body/dot_general | solution.py:14
  147.8 3.0 %fusion.158 = bf16[512,512]{0,1:T(8,128)(2,1)} fusion(bf16[512,512]{1,0:T(8,128)(2,1)} %convolution_convert_fusion.22, f32[512,512]{1,0:T(8,128)S(1)} %fusion.157), kind=kOutput, calls=%fused_computation.28.clone.1 | convolution fusion | flops 538705920 | bytes 2097152 | tf_op jit(solution)/shard_map/while/body/dot_general | solution.py:14
  150.8 2.9 %convolution_convert_fusion.23 = bf16[512,512]{1,0:T(8,128)(2,1)} fusion(bf16[512,512]{0,1:T(8,128)(2,1)} %fusion.158, f32[512,512]{0,1:T(8,128)S(1)} %get-tuple-element.140, f32[]{:T(128)S(6)} %mul.308, f32[]{:T(128)S(6)} %div.78, f32[512,512]{0,1:T(8,128)} %copy.87), kind=kOutput, calls=%fused_computation.22.clone.1 | convolution fusion | flops 540278784 | bytes 3145736 | tf_op jit(solution)/shard_map/while/body/dot_general | solution.py:14
  155.8 3.5 %fusion.161 = bf16[1,512,512]{1,2,0:T(8,128)(2,1)} fusion(bf16[1,512,512]{1,2,0:T(8,128)(2,1)S(1)} %copy.86, bf16[512,512]{1,0:T(8,128)(2,1)} %convolution_convert_fusion.23, bf16[512,512]{1,0:T(8,128)(2,1)} %convolution_convert_fusion.26, pred[]{:T(512)} %and_reduce_fusion.2, bf16[2,512,512]{2,1,0:T(8,128)(2,1)} %get-tuple-element.180, s32[]{:T(128)} %select_n.151), kind=kOutput, calls=%fused_computation.33.clone.1 | convolution fusion | flops 537657344 | bytes 2622464 | tf_op jit(solution)/shard_map/while/body/dot_general | solution.py:52
  161.4 3.9 %fusion.156 = (f32[2,512,512]{1,2,0:T(8,128)}, f32[2,512,512]{1,2,0:T(8,128)}) fusion(f32[2,512,512]{1,2,0:T(8,128)} %get-tuple-element.162, s32[]{:T(128)} %select_n.151, f32[512,512]{0,1:T(8,128)S(1)} %get-tuple-element.139, pred[]{:T(512)} %and_reduce_fusion.2, f32[2,512,512]{1,2,0:T(8,128)} %get-tuple-element.161, ...), kind=kLoop, calls=%fused_computation.39.clone.1 | loop fusion | flops 524288 | bytes 6292480 | tf_op jit(solution)/shard_map/while/body/scatter | solution.py:102
  166.0 2.1 abs_reduce_fusion.4
  172.3 2.9 %fusion.160 = bf16[512,512]{0,1:T(8,128)(2,1)} fusion(bf16[512,512]{1,0:T(8,128)(2,1)} %convolution_convert_fusion.25, f32[512,512]{1,0:T(8,128)S(1)} %fusion.159), kind=kOutput, calls=%fused_computation.29.clone.1 | convolution fusion | flops 538705920 | bytes 2097152 | tf_op jit(solution)/shard_map/while/body/dot_general | solution.py:14
  175.4 2.6 %convolution_convert_fusion.26 = bf16[512,512]{1,0:T(8,128)(2,1)} fusion(bf16[512,512]{0,1:T(8,128)(2,1)} %fusion.160, f32[512,512]{0,1:T(8,128)S(1)} %get-tuple-element.139, f32[]{:T(128)S(6)} %mul.309, f32[]{:T(128)S(6)} %div.79, f32[512,512]{0,1:T(8,128)S(1)} %copy.88), kind=kOutput, calls=%fused_computation.16.clone.1 | convolution fusion | flops 540278784 | bytes 3145736 | tf_op jit(solution)/shard_map/while/body/dot_general | solution.py:14
  182.6 2.1 fusion.157
  186.1 2.8 %convolution_convert_fusion.22 = bf16[512,512]{1,0:T(8,128)(2,1)} fusion(f32[512,512]{0,1:T(8,128)} %copy.87), kind=kOutput, calls=%fused_computation.24.clone.1 | convolution fusion | flops 270008320 | bytes 1572864 | tf_op jit(solution)/shard_map/while/body/dot_general | solution.py:14
  189.0 3.0 %fusion.158 = bf16[512,512]{0,1:T(8,128)(2,1)} fusion(bf16[512,512]{1,0:T(8,128)(2,1)} %convolution_convert_fusion.22, f32[512,512]{1,0:T(8,128)S(1)} %fusion.157), kind=kOutput, calls=%fused_computation.28.clone.1 | convolution fusion | flops 538705920 | bytes 2097152 | tf_op jit(solution)/shard_map/while/body/dot_general | solution.py:14
  192.0 2.9 %convolution_convert_fusion.23 = bf16[512,512]{1,0:T(8,128)(2,1)} fusion(bf16[512,512]{0,1:T(8,128)(2,1)} %fusion.158, f32[512,512]{0,1:T(8,128)S(1)} %get-tuple-element.140, f32[]{:T(128)S(6)} %mul.308, f32[]{:T(128)S(6)} %div.78, f32[512,512]{0,1:T(8,128)} %copy.87), kind=kOutput, calls=%fused_computation.22.clone.1 | convolution fusion | flops 540278784 | bytes 3145736 | tf_op jit(solution)/shard_map/while/body/dot_general | solution.py:14
  196.9 3.5 %fusion.161 = bf16[1,512,512]{1,2,0:T(8,128)(2,1)} fusion(bf16[1,512,512]{1,2,0:T(8,128)(2,1)S(1)} %copy.86, bf16[512,512]{1,0:T(8,128)(2,1)} %convolution_convert_fusion.23, bf16[512,512]{1,0:T(8,128)(2,1)} %convolution_convert_fusion.26, pred[]{:T(512)} %and_reduce_fusion.2, bf16[2,512,512]{2,1,0:T(8,128)(2,1)} %get-tuple-element.180, s32[]{:T(128)} %select_n.151), kind=kOutput, calls=%fused_computation.33.clone.1 | convolution fusion | flops 537657344 | bytes 2622464 | tf_op jit(solution)/shard_map/while/body/dot_general | solution.py:52
  202.6 3.9 %fusion.156 = (f32[2,512,512]{1,2,0:T(8,128)}, f32[2,512,512]{1,2,0:T(8,128)}) fusion(f32[2,512,512]{1,2,0:T(8,128)} %get-tuple-element.162, s32[]{:T(128)} %select_n.151, f32[512,512]{0,1:T(8,128)S(1)} %get-tuple-element.139, pred[]{:T(512)} %and_reduce_fusion.2, f32[2,512,512]{1,2,0:T(8,128)} %get-tuple-element.161, ...), kind=kLoop, calls=%fused_computation.39.clone.1 | loop fusion | flops 524288 | bytes 6292480 | tf_op jit(solution)/shard_map/while/body/scatter | solution.py:102
  207.1 2.3 copy.72
  209.4 4.8 %all-to-all-start.2 = ((bf16[2,16,32,512]{3,2,0,1:T(8,128)(2,1)}), bf16[2,16,32,512]{3,2,0,1:T(8,128)(2,1)S(1)}, u32[]{:S(2)}, u32[]{:S(2)}) async-start(bf16[2,16,32,512]{3,2,0,1:T(8,128)(2,1)} %copy.72), calls=%async_computation.3 | async-start | bytes 2097152 | tf_op jit(solution)/shard_map/all_to_all | solution.py:113
  214.3 18.1 %all-to-all-done.2 = bf16[2,16,32,512]{3,2,0,1:T(8,128)(2,1)S(1)} async-done(((bf16[2,16,32,512]{3,2,0,1:T(8,128)(2,1)}), bf16[2,16,32,512]{3,2,0,1:T(8,128)(2,1)S(1)}, u32[]{:S(2)}, u32[]{:S(2)}) %all-to-all-start.2) | async-done | bytes 1048608 | tf_op jit(solution)/shard_map/all_to_all | solution.py:113
  235.9 3.9 %all-to-all-start.3 = ((bf16[16,32,512]{2,1,0:T(8,128)(2,1)}), bf16[16,32,512]{2,1,0:T(8,128)(2,1)S(1)}, u32[]{:S(2)}, u32[]{:S(2)}) async-start(bf16[16,32,512]{2,1,0:T(8,128)(2,1)} %broadcast_select_fusion), calls=%async_computation.4 | async-start | bytes 1048576 | tf_op jit(solution)/shard_map/all_to_all | solution.py:116
  241.6 2.9 %copy.75 = f32[2,512,512]{2,1,0:T(8,128)} copy(f32[2,512,512]{1,2,0:T(8,128)} %get-tuple-element.76) | data formatting | bytes 4194304 | tf_op jit(solution)/shard_map/while | solution.py:106
  244.4 7.7 %all-to-all-done.3 = bf16[16,32,512]{2,1,0:T(8,128)(2,1)S(1)} async-done(((bf16[16,32,512]{2,1,0:T(8,128)(2,1)}), bf16[16,32,512]{2,1,0:T(8,128)(2,1)S(1)}, u32[]{:S(2)}, u32[]{:S(2)}) %all-to-all-start.3) | async-done | bytes 524320 | tf_op jit(solution)/shard_map/all_to_all | solution.py:116
  (66 shorter events, 40.8 us)
Async XLA Ops:
  7.2 1.0 copy-start
  7.2 75.6 %reduce-scatter.2.cloned.1.call-start = ((), (), s32[]{:S(2)}) async-start(), calls=%async_computation.5 | async-start | bytes 8912896 | tf_op jit(solution)/shard_map/reduce_scatter | solution.py:63
  15.9 0.7 copy-start.4
  82.8 16.9 %all-to-all-start = ((bf16[16,32,512]{2,1,0:T(8,128)(2,1)}), bf16[16,32,512]{2,1,0:T(8,128)(2,1)S(1)}, u32[]{:S(2)}, u32[]{:S(2)}) async-start(bf16[16,32,512]{2,1,0:T(8,128)(2,1)} %bitcast.120), calls=%async_computation.1 | async-start | bytes 1048576 | tf_op jit(solution)/shard_map/all_to_all | solution.py:81
  100.5 6.0 %copy-start.2 = (f32[1,2,512,512]{3,2,1,0:T(8,128)S(1)}, f32[1,2,512,512]{3,2,1,0:T(8,128)}, u32[]{:S(2)}) copy-start(f32[1,2,512,512]{3,2,1,0:T(8,128)} %param.16) | copy-start | bytes 6291460
  101.5 20.3 %all-to-all-start.1 = ((bf16[2,16,32,512]{3,2,0,1:T(8,128)(2,1)}), bf16[2,16,32,512]{3,2,0,1:T(8,128)(2,1)S(1)}, u32[]{:S(2)}, u32[]{:S(2)}) async-start(bf16[2,16,32,512]{3,2,0,1:T(8,128)(2,1)} %copy.69), calls=%async_computation.2 | async-start | bytes 2097152 | tf_op jit(solution)/shard_map/all_to_all | solution.py:90
  111.2 12.8 %copy-start.3 = (s32[3]{0:T(128)S(1)}, s32[3]{0:T(128)}, u32[]{:S(2)}) copy-start(s32[3]{0:T(128)} %constant.135.clone.1) | copy-start | bytes 40
  209.4 23.0 %all-to-all-start.2 = ((bf16[2,16,32,512]{3,2,0,1:T(8,128)(2,1)}), bf16[2,16,32,512]{3,2,0,1:T(8,128)(2,1)S(1)}, u32[]{:S(2)}, u32[]{:S(2)}) async-start(bf16[2,16,32,512]{3,2,0,1:T(8,128)(2,1)} %copy.72), calls=%async_computation.3 | async-start | bytes 2097152 | tf_op jit(solution)/shard_map/all_to_all | solution.py:113
  232.5 7.2 %copy-start.1 = (f32[2,512,512]{1,2,0:T(8,128)S(1)}, f32[2,512,512]{1,2,0:T(8,128)}, u32[]{:S(2)}) copy-start(f32[2,512,512]{1,2,0:T(8,128)} %get-tuple-element.75) | copy-start | bytes 6291460
  235.9 16.3 %all-to-all-start.3 = ((bf16[16,32,512]{2,1,0:T(8,128)(2,1)}), bf16[16,32,512]{2,1,0:T(8,128)(2,1)S(1)}, u32[]{:S(2)}, u32[]{:S(2)}) async-start(bf16[16,32,512]{2,1,0:T(8,128)(2,1)} %broadcast_select_fusion), calls=%async_computation.4 | async-start | bytes 1048576 | tf_op jit(solution)/shard_map/all_to_all | solution.py:116
Sparse Core Ops, SparseCore 0:
  16.1 66.6 reduce-scatter.1
where the time goes:
time: 261 us; the launch traced here: 260 us
  waiting for transfers between devices  112 us (43%)
  matrix products  63.9 us (24%)
  local copies, waits for them, and re-layouts  29.9 us (11%)
  starting transfers between devices  19.7 us (8%)
  other arithmetic  14.7 us (6%)
  between operations  14.2 us (5%)
  loops' own time  5.37 us (2%)
    reduce_scatter x1, waiting for transfers between devices, shards(): lax.psum_scatter(lax.dot_general(activations, cotangents, (((0,), (0,)),...  66.1 us
    dot_general x20, matrix products, matmul_bf(): jnp.dot(left_op.astype(jnp.bfloat16), right_op.astype(jnp.bfloat16), pref...  40.7 us
    all_to_all x1, waiting for transfers between devices, shards(): lax.all_to_all(sending, 'prec', split_axis=1, concat_axis=1, tiled=True)  18.1 us
    all_to_all x1, waiting for transfers between devices, shards(): lax.all_to_all(outgoing, 'prec', split_axis=1, concat_axis=2, tiled=True)  10.7 us
    all_to_all x1, waiting for transfers between devices, shards(): lax.all_to_all(pieces, 'prec', split_axis=0, concat_axis=0, tiled=True)  9.46 us
    dot_general x1, matrix products, shards(): lax.dot_general(activations, cotangents, (((0,), (0,)), ((), ())), prefer...  7.79 us
    scatter x2, other arithmetic, per_slot(): right_acc.at[slot_pos].set(right_one)  7.78 us
    all_to_all x1, waiting for transfers between devices, shards(): lax.all_to_all(per_block, 'prec', split_axis=0, concat_axis=1, tiled=True)  7.73 us
  transfers between devices with their start and end apart: 5, of which 5 were waited for; matrix products, arithmetic and copies ran while one was open for 4% of the time, Pallas kernels for 0%

commit v1 on v0

v1 whole, which is shorter than its diff:
```python
import functools

import jax
import jax.numpy as jnp
from jax import lax
from jax.experimental import pallas as pl
from jax.experimental.pallas import tpu as pltpu
from jax.sharding import PartitionSpec as P

CAP = 2
HALVES = 2
SUBS = 2
TILE = 128
UNIT = 16
DECAY = 0.95
BF = jnp.bfloat16
F32 = jnp.float32


def nn(a, b):
    return jnp.dot(a, b, preferred_element_type=F32)


def nt(a, b):
    return lax.dot_general(a, b, (((1,), (1,)), ((), ())), preferred_element_type=F32)


def tn(a, b):
    return lax.dot_general(a, b, (((0,), (0,)), ((), ())), preferred_element_type=F32)


def upper_tiles(blk):
    side = blk // TILE
    return [(i, j) for i in range(side) for j in range(i, side)]


def five_minus(m):
    rows = lax.broadcasted_iota(jnp.int32, m.shape, 0)
    cols = lax.broadcasted_iota(jnp.int32, m.shape, 1)
    return jnp.where(rows == cols, 1.25, 0.0) - 0.25 * m


def inverse_root(a_ref, out_ref, f_ref):
    a = a_ref[...]
    top = jnp.max(jnp.sum(jnp.abs(a), axis=0, keepdims=True), axis=1, keepdims=True) + 1e-06
    z = 2.5 / top
    m0 = a * z
    m0b = m0.astype(BF)
    f0b = five_minus(m0).astype(BF)
    sq = nn(f0b, f0b).astype(BF)
    quad = nn(sq, sq).astype(BF)
    f_ref[...] = five_minus(nn(quad, m0b))
    f1b = f_ref[...].astype(BF)
    s1 = nn(f1b, f1b)
    u = (5.0 * f_ref[...] - 4.0 * s1).astype(BF)
    s1 = s1.astype(BF)
    q1 = nn(s1, s1).astype(BF)
    h = (1.25 * f_ref[...] - 0.25 * nn(q1, u)).astype(BF)
    out_ref[...] = (nn(f0b, h) * jnp.sqrt(jnp.sqrt(z))).astype(BF)


def travel_kernel(
    nd, npr,
    own_ref, act_ref, cot_ref, left_ref, right_ref,
    half_ref, xr_ref, slots_ref,
    a_all, cbuf, ct, stat, pk1, st1, pk2, st2, rs_out, rs_in, part, gt, gsa, gsb, g1a, g1b, pk3a, pk3b, sla, slb, mats, f_scr, xl,
    table,
    loc_sem, stat_sem, xs, xr, rss, rsr, s1s, s1r, s2s, s2r, g1s, g1r, g2s, g2r,
):
    nz = nd // 2
    steps = nz - 1
    tok, blk = cot_ref.shape
    hrow = blk // HALVES
    drow = hrow // 2
    srow = drow // SUBS
    grow = hrow // npr
    d = lax.axis_index("dp")
    p = lax.axis_index("prec")
    z = d // 2
    core = d % 2
    twin = d + 1 - 2 * core
    up = (d + 2) % nd
    down = (d + nd - 2) % nd
    MESH = pl.DeviceIdType.MESH
    g1 = (g1a, g1b)
    gs = (gsa, gsb)
    pk3 = (pk3a, pk3b)
    landed = (sla, slb)
    tiles = upper_tiles(blk)

    def remote(src, dst, ssem, rsem, **where):
        return pltpu.make_async_remote_copy(
            src_ref=src, dst_ref=dst, send_sem=ssem, recv_sem=rsem,
            device_id=where, device_id_type=MESH,
        )

    def peers(fn):
        @pl.loop(1, npr)
        def _(s):
            fn((p + s) % npr)

    def order(k):
        if isinstance(k, int) and k == nz - 1:
            return z
        return (z + nz + (2 * (k % 2) - 1) * (k // 2 + 1)) % nz

    def own_rows(k):
        dest = order(k)
        cols = pl.ds(pl.multiple_of((2 * dest + core) * blk, blk), blk)
        return pltpu.make_async_copy(
            act_ref.at[:, cols], a_all.at[dest, pl.ds(0, tok)], loc_sem.at[k]
        )

    def twin_rows(k):
        dest = order(k)
        cols = pl.ds(pl.multiple_of((2 * dest + 1 - core) * blk, blk), blk)
        return remote(
            act_ref.at[:, cols], a_all.at[dest, pl.ds(tok, tok)], xs.at[k], xr.at[k], dp=twin
        )

    own_cot = pltpu.make_async_copy(cot_ref, cbuf.at[pl.ds(0, tok)], loc_sem.at[nz])
    twin_cot = remote(cot_ref, cbuf.at[pl.ds(tok, tok)], xs.at[nz], xr.at[nz], dp=twin)
    left_in = pltpu.make_async_copy(left_ref.at[0], stat.at[0], stat_sem.at[0])
    right_in = pltpu.make_async_copy(right_ref.at[0], stat.at[1], stat_sem.at[1])

    own_cot.start()

    @pl.loop(0, nz - 1)
    def _(k):
        own_rows(k).start()

    own_rows(nz - 1).start()
    left_in.start()
    right_in.start()

    barrier = pltpu.get_barrier_semaphore()
    for other in (twin, up, down):
        pl.semaphore_signal(barrier, inc=1, device_id={"dp": other}, device_id_type=MESH)
    peers(
        lambda t: pl.semaphore_signal(barrier, inc=1, device_id={"prec": t}, device_id_type=MESH)
    )
    pl.semaphore_wait(barrier, 3 + npr - 1)

    twin_cot.start()

    @pl.loop(0, nz - 1)
    def _(k):
        twin_rows(k).start()

    twin_rows(nz - 1).start()

    def stat_one(t):
        return remote(
            pk1.at[t], st1.at[pl.ds(p * CAP, CAP)], s1s.at[t], s1r.at[p], prec=t
        )

    def stat_one_from(u):
        return remote(
            pk1.at[u], st1.at[pl.ds(u * CAP, CAP)], s1s.at[u], s1r.at[u], prec=u
        )

    def stat_two(t):
        return remote(pk2.at[t], st2.at[p], s2s.at[t], s2r.at[p], prec=t)

    def stat_two_from(u):
        return remote(pk2.at[u], st2.at[u], s2s.at[u], s2r.at[u], prec=u)

    def pack_stats():
        left_in.wait()
        right_in.wait()

        @pl.loop(0, CAP)
        def _(slot):
            for m in range(2):
                for n, (i, j) in enumerate(tiles):
                    for u in range(TILE // UNIT):
                        at = (m * len(tiles) + n) * (TILE // UNIT) + u
                        pk1[at % npr, slot, pl.ds(at // npr * UNIT, UNIT), :] = stat[
                            m, slot, pl.ds(i * TILE + u * UNIT, UNIT), pl.ds(j * TILE, TILE)
                        ].astype(BF)

        peers(lambda t: stat_one(t).start())

    def turn_stats():
        peers(lambda u: stat_one_from(u).wait_recv())
        st1[pl.ds(p * CAP, CAP)] = pk1[p]

        @pl.loop(0, npr)
        def _(c):
            pk2[c] = st1[own_ref[0, c]]

        peers(lambda t: stat_two(t).start())

    def unpack_stats():
        peers(lambda u: stat_two_from(u).wait_recv())
        st2[p] = pk2[p]
        for m in range(2):
            for n, (i, j) in enumerate(tiles):
                rows = []
                for u in range(TILE // UNIT):
                    at = (m * len(tiles) + n) * (TILE // UNIT) + u
                    rows.append(st2[at % npr, pl.ds(at // npr * UNIT, UNIT), :])
                tile = jnp.concatenate(rows, axis=0).astype(F32) * DECAY
                mats[m, pl.ds(i * TILE, TILE), pl.ds(j * TILE, TILE)] = tile
                if i != j:
                    mats[m, pl.ds(j * TILE, TILE), pl.ds(i * TILE, TILE)] = tile.T

    def make_table():
        @pl.loop(0, npr * CAP)
        def _(q):
            def pick(c, found):
                return jnp.where(own_ref[0, c] == q, c, found)

            table[q] = lax.fori_loop(0, npr, pick, jnp.int32(0))

    def grad_one(h, t):
        return remote(
            gs[h].at[t], g1[h].at[p],
            g1s.at[h, t], g1r.at[h, p], prec=t,
        )

    def grad_one_from(h, u):
        return remote(
            gs[h].at[u], g1[h].at[u],
            g1s.at[h, u], g1r.at[h, u], prec=u,
        )

    def grad_two(h, t):
        return remote(
            pk3[h].at[t], landed[h].at[p],
            g2s.at[h, t], g2r.at[h, p], prec=t,
        )

    def grad_two_from(h, u):
        return remote(
            pk3[h].at[u], landed[h].at[u],
            g2s.at[h, u], g2r.at[h, u], prec=u,
        )

    def ring(it, way, sub):
        return remote(
            rs_out.at[it, way, sub], rs_in.at[it, way, sub],
            rss.at[it, way * SUBS + sub], rsr.at[it, way * SUBS + sub],
            dp=up if way == 0 else down,
        )

    def finish_half(h):
        base = h * hrow
        last = h * steps + steps - 1
        for way in range(2):
            rows = pl.ds(base + way * drow, drow)
            part[way] = nn(ct[rows, :], a_all[z])
            for sub in range(SUBS):
                ring(last, way, sub).wait_recv()
                done = (
                    part[way, pl.ds(sub * srow, srow), :] + rs_in[last, way, sub].astype(F32)
                ).astype(BF)
                gt[pl.ds(base + way * drow + sub * srow, srow), :] = done
                first = (way * drow + sub * srow) // grow
                gs[h][pl.ds(first, srow // grow)] = done.reshape(srow // grow, grow, blk)
        peers(lambda t: grad_one(h, t).start())

    def turn_half(h):
        peers(lambda u: grad_one_from(h, u).wait_recv())
        g1[h][p] = gs[h][p]

        @pl.loop(0, npr)
        def _(o):
            for slot in range(CAP):
                pk3[h][o, slot] = g1[h][table[o * CAP + slot]]

        peers(lambda t: grad_two(h, t).start())

    own_cot.wait()
    twin_cot.wait_recv()
    ct[...] = cbuf[...].T

    @pl.loop(0, nz - 1)
    def _(k):
        own_rows(k).wait()
        twin_rows(k).wait_recv()

    own_rows(nz - 1).wait()
    twin_rows(nz - 1).wait_recv()

    @pl.loop(0, HALVES * steps)
    def _(it):
        h = it // steps
        s = it % steps

        for way in range(2):
            dest = (z + nz - 1 - s) % nz if way == 0 else (z + 1 + s) % nz
            rows = pl.ds(pl.multiple_of(h * hrow + way * drow, drow), drow)
            part[way] = nn(ct[rows, :], a_all[dest])
        for sub in range(SUBS):
            for way in range(2):
                rows = pl.ds(sub * srow, srow)

                @pl.when(s == 0)
                def _():
                    rs_out[it, way, sub] = part[way, rows, :].astype(BF)

                @pl.when(s > 0)
                def _():
                    ring(it - 1, way, sub).wait_recv()
                    rs_out[it, way, sub] = (
                        part[way, rows, :] + rs_in[it - 1, way, sub].astype(F32)
                    ).astype(BF)

                ring(it, way, sub).start()

        @pl.when(it == 0)
        def _():
            pack_stats()

        @pl.when(it == 1)
        def _():
            make_table()

        @pl.when(it == steps)
        def _():
            finish_half(0)

        @pl.when(it == steps + 1)
        def _():
            turn_stats()

        @pl.when(it == steps + steps // 2)
        def _():
            turn_half(0)

        @pl.when(it == 2 * steps - 1)
        def _():
            unpack_stats()

    finish_half(1)
    g = gt[...]
    mats[1] += nt(g, g) * (1.0 / blk)
    inverse_root(mats.at[1], xr_ref, f_scr)
    turn_half(1)
    mats[0] += tn(g, g) * (1.0 / blk)
    inverse_root(mats.at[0], xl, f_scr)
    half_ref[...] = nt(xl[...], gt[...]).astype(BF)

    for h in range(HALVES):
        peers(lambda u, h=h: grad_two_from(h, u).wait_recv())
        landed[h][p] = pk3[h][p]
        slots_ref[h] = landed[h][...]

    twin_cot.wait_send()

    @pl.loop(0, nz - 1)
    def _(k):
        twin_rows(k).wait_send()

    twin_rows(nz - 1).wait_send()

    @pl.loop(0, HALVES * steps)
    def _(it):
        for way in range(2):
            for sub in range(SUBS):
                ring(it, way, sub).wait_send()

    def sent(t):
        stat_one(t).wait_send()
        stat_two(t).wait_send()
        for h in range(HALVES):
            grad_one(h, t).wait_send()
            grad_two(h, t).wait_send()

    peers(sent)


def fresh_kernel(parts, own_ref, half_ref, xr_ref, slots_ref, left_ref, right_ref,
                 upd_ref, lout_ref, rout_ref, g_scr):
    step = pl.program_id(0)
    slot = step // parts
    piece = step % parts
    blk = half_ref.shape[0]
    rows = blk // parts
    q = lax.axis_index("prec") * CAP + slot
    named = jnp.int32(0)
    for c in range(own_ref.shape[1]):
        named = named + (own_ref[0, c] == q).astype(jnp.int32)

    @pl.when(step == 0)
    def _():
        upd_ref[...] = nn(half_ref[...], xr_ref[...]).astype(BF)

    @pl.when(named > 0)
    def _():
        at = pl.multiple_of(piece * rows, rows)
        g = slots_ref[...].reshape(blk, blk)
        g_scr[...] = g
        lout_ref[0, 0] = DECAY * left_ref[0, 0] + tn(g_scr[:, pl.ds(at, rows)], g) * (1.0 / blk)
        rout_ref[0, 0] = DECAY * right_ref[0, 0] + nt(g_scr[pl.ds(at, rows), :], g) * (1.0 / blk)

    @pl.when(named == 0)
    def _():
        lout_ref[...] = left_ref[...]
        rout_ref[...] = right_ref[...]


def shards(activations, cotangents, owner_slots, left_stats, right_stats):
    nd = lax.axis_size("dp")
    npr = lax.axis_size("prec")
    tok, blk = cotangents.shape
    nz = nd // 2
    its = HALVES * (nz - 1)
    hrow = blk // HALVES
    srow = hrow // 2 // SUBS
    grow = hrow // npr
    srows = 2 * len(upper_tiles(blk)) * TILE // npr
    dma = pltpu.SemaphoreType.DMA
    vmem = pl.BlockSpec(memory_space=pltpu.VMEM)
    far = pl.BlockSpec(memory_space=pltpu.HBM)
    half, xr, slots = pl.pallas_call(
        functools.partial(travel_kernel, nd, npr),
        out_shape=[
            jax.ShapeDtypeStruct((blk, blk), BF),
            jax.ShapeDtypeStruct((blk, blk), BF),
            jax.ShapeDtypeStruct((HALVES, npr, CAP, grow, blk), BF),
        ],
        in_specs=[pl.BlockSpec(memory_space=pltpu.SMEM)] + [far] * 4,
        out_specs=[vmem] * 3,
        scratch_shapes=[
            pltpu.VMEM((nz, 2 * tok, blk), BF),
            pltpu.VMEM((2 * tok, blk), BF),
            pltpu.VMEM((blk, 2 * tok), BF),
            pltpu.VMEM((2, CAP, blk, blk), F32),
            pltpu.VMEM((npr, CAP, srows, TILE), BF),
            pltpu.VMEM((npr * CAP, srows, TILE), BF),
            pltpu.VMEM((npr, srows, TILE), BF),
            pltpu.VMEM((npr, srows, TILE), BF),
            pltpu.VMEM((its, 2, SUBS, srow, blk), BF),
            pltpu.VMEM((its, 2, SUBS, srow, blk), BF),
            pltpu.VMEM((2, hrow // 2, blk), F32),
            pltpu.VMEM((blk, blk), BF),
            pltpu.VMEM((npr, grow, blk), BF),
            pltpu.VMEM((npr, grow, blk), BF),
            pltpu.VMEM((npr, grow, blk), BF),
            pltpu.VMEM((npr, grow, blk), BF),
            pltpu.VMEM((npr, CAP, grow, blk), BF),
            pltpu.VMEM((npr, CAP, grow, blk), BF),
            pltpu.VMEM((npr, CAP, grow, blk), BF),
            pltpu.VMEM((npr, CAP, grow, blk), BF),
            pltpu.VMEM((2, blk, blk), F32),
            pltpu.VMEM((blk, blk), F32),
            pltpu.VMEM((blk, blk), BF),
            pltpu.SMEM((npr * CAP,), jnp.int32),
            dma((nz + 1,)),
            dma((2,)),
            dma((nz + 1,)),
            dma((nz + 1,)),
            dma((its, 2 * SUBS)),
            dma((its, 2 * SUBS)),
            dma((npr,)),
            dma((npr,)),
            dma((npr,)),
            dma((npr,)),
            dma((HALVES, npr)),
            dma((HALVES, npr)),
            dma((HALVES, npr)),
            dma((HALVES, npr)),
        ],
        compiler_params=pltpu.CompilerParams(
            collective_id=0, has_side_effects=True, vmem_limit_bytes=60 * 1024 * 1024
        ),
        name="travel",
    )(owner_slots, activations, cotangents, left_stats, right_stats)

    parts = 2
    rows = blk // parts
    stat_spec = pl.BlockSpec((1, 1, rows, blk), lambda i: (0, i // parts, i % parts, 0))
    whole = pl.BlockSpec((blk, blk), lambda i: (0, 0))
    update, left_out, right_out = pl.pallas_call(
        functools.partial(fresh_kernel, parts),
        grid=(CAP * parts,),
        out_shape=[
            jax.ShapeDtypeStruct((blk, blk), BF),
            jax.ShapeDtypeStruct(left_stats.shape, F32),
            jax.ShapeDtypeStruct(right_stats.shape, F32),
        ],
        in_specs=[
            pl.BlockSpec(memory_space=pltpu.SMEM),
            whole,
            whole,
            pl.BlockSpec((HALVES, npr, 1, grow, blk), lambda i: (0, 0, i // parts, 0, 0)),
            stat_spec,
            stat_spec,
        ],
        out_specs=[whole, stat_spec, stat_spec],
        scratch_shapes=[pltpu.VMEM((blk, blk), BF)],
        compiler_params=pltpu.CompilerParams(vmem_limit_bytes=60 * 1024 * 1024),
        name="fresh",
    )(owner_slots, half, xr, slots, left_stats, right_stats)
    return (update, left_out, right_out)


def solution(mesh):
    placed = (
        P("dp", None),
        P("dp", "prec"),
        P("dp", None),
        P("dp", "prec", None, None),
        P("dp", "prec", None, None),
    )
    return jax.shard_map(
        shards,
        mesh=mesh,
        in_specs=placed,
        out_specs=(P("dp", "prec"), P("dp", "prec", None, None), P("dp", "prec", None, None)),
        check_vma=False,
    )
```

time: 261 us -> 97.8 us (0.37)
  the two profiles are of different devices: /device:TPU:64 before, /device:TPU:24 now
where the time goes in v1:
time: 97.8 us; the launch traced here: 96.7 us
  Pallas kernels  96.1 us (98%)
    pallas_call x1, Pallas kernels, shards(): pl.pallas_call(functools.partial(travel_kernel, nd, npr), out_shape=[jax....  90.1 us
    pallas_call x1, Pallas kernels, shards(): pl.pallas_call(functools.partial(fresh_kernel, parts), grid=(CAP * parts,...  6.01 us

profile of v1, /device:TPU:24, one launch (start us, length us, event | category | flops | bytes accessed | tf_op | source)
XLA Modules:
  0.0 96.7 jit_solution(11319671636832447053)
XLA Ops:
  0.6 90.1 %travel.1 = (bf16[512,512]{1,0:T(8,128)(2,1)}, bf16[512,512]{1,0:T(8,128)(2,1)}, bf16[2,16,2,16,512]{4,3,2,1,0:T(8,128)(2,1)}) custom-call(s32[1,16]{1,0:T(1,128)} %own_ref.3, bf16[256,8192]{1,0:T(8,128)(2,1)} %act_ref.1, bf16[256,512]{1,0:T(8,128)(2,1)} %cot_ref.1, f32[1,2,512,512]{3,2,1,0:T(8,128)} %left_ref.3, f32[1,2,512,512]{3,2,1,0:T(8,128)} %right_ref.3), custom_call_target="tpu_custom_call" | custom-call | tf_op jit(solution)/shard_map/travel/pallas_call | solution.py:417
  90.7 6.0 %fresh.1 = (bf16[512,512]{1,0:T(8,128)(2,1)}, f32[1,2,512,512]{3,2,1,0:T(8,128)}, f32[1,2,512,512]{3,2,1,0:T(8,128)}) custom-call(s32[1,16]{1,0:T(1,128)} %own_ref.3, bf16[512,512]{1,0:T(8,128)(2,1)} %get-tuple-element.6.half_ref, bf16[512,512]{1,0:T(8,128)(2,1)} %get-tuple-element.7.xr_ref, bf16[2,16,2,16,512]{4,3,2,1,0:T(8,128)(2,1)} %get-tuple-element.8.slots_ref, ...), custom_call_target="tpu_custom_call" | custom-call | tf_op jit(solution)/shard_map/fresh/pallas_call | solution.py:476

commit v2 on v1

--- a/solution.py
+++ b/solution.py
@@ -68,11 +68,10 @@
     loc_sem, stat_sem, xs, xr, rss, rsr, s1s, s1r, s2s, s2r, g1s, g1r, g2s, g2r,
 ):
     nz = nd // 2
-    steps = nz - 1
+    arc = nz // 2
     tok, blk = cot_ref.shape
     hrow = blk // HALVES
-    drow = hrow // 2
-    srow = drow // SUBS
+    srow = hrow // SUBS
     grow = hrow // npr
     d = lax.axis_index("dp")
     p = lax.axis_index("prec")
@@ -100,22 +99,20 @@
             fn((p + s) % npr)
 
     def order(k):
-        if isinstance(k, int) and k == nz - 1:
-            return z
-        return (z + nz + (2 * (k % 2) - 1) * (k // 2 + 1)) % nz
+        return (z + nz + (2 * (k % 2) - 1) * (arc - (k + 1) // 2)) % nz
 
     def own_rows(k):
         dest = order(k)
         cols = pl.ds(pl.multiple_of((2 * dest + core) * blk, blk), blk)
         return pltpu.make_async_copy(
-            act_ref.at[:, cols], a_all.at[dest, pl.ds(0, tok)], loc_sem.at[k]
+            act_ref.at[:, cols], a_all.at[k, pl.ds(0, tok)], loc_sem.at[k]
         )
 
     def twin_rows(k):
         dest = order(k)
         cols = pl.ds(pl.multiple_of((2 * dest + 1 - core) * blk, blk), blk)
         return remote(
-            act_ref.at[:, cols], a_all.at[dest, pl.ds(tok, tok)], xs.at[k], xr.at[k], dp=twin
+            act_ref.at[:, cols], a_all.at[k, pl.ds(tok, tok)], xs.at[k], xr.at[k], dp=twin
         )
 
     own_cot = pltpu.make_async_copy(cot_ref, cbuf.at[pl.ds(0, tok)], loc_sem.at[nz])
@@ -123,13 +120,20 @@
     left_in = pltpu.make_async_copy(left_ref.at[0], stat.at[0], stat_sem.at[0])
     right_in = pltpu.make_async_copy(right_ref.at[0], stat.at[1], stat_sem.at[1])
 
+    def make_table():
+        @pl.loop(0, npr * CAP)
+        def _(q):
+            def pick(c, found):
+                return jnp.where(own_ref[0, c] == q, c, found)
+
+            table[q] = lax.fori_loop(0, npr, pick, jnp.int32(0))
+
     own_cot.start()
 
-    @pl.loop(0, nz - 1)
+    @pl.loop(0, nz)
     def _(k):
         own_rows(k).start()
 
-    own_rows(nz - 1).start()
     left_in.start()
     right_in.start()
 
@@ -139,15 +143,14 @@
     peers(
         lambda t: pl.semaphore_signal(barrier, inc=1, device_id={"prec": t}, device_id_type=MESH)
     )
+    make_table()
     pl.semaphore_wait(barrier, 3 + npr - 1)
 
     twin_cot.start()
 
-    @pl.loop(0, nz - 1)
+    @pl.loop(0, nz)
     def _(k):
         twin_rows(k).start()
-
-    twin_rows(nz - 1).start()
 
     def stat_one(t):
         return remote(
@@ -178,8 +181,6 @@
                         pk1[at % npr, slot, pl.ds(at // npr * UNIT, UNIT), :] = stat[
                             m, slot, pl.ds(i * TILE + u * UNIT, UNIT), pl.ds(j * TILE, TILE)
                         ].astype(BF)
-
-        peers(lambda t: stat_one(t).start())
 
     def turn_stats():
         peers(lambda u: stat_one_from(u).wait_recv())
@@ -205,14 +206,6 @@
                 if i != j:
                     mats[m, pl.ds(j * TILE, TILE), pl.ds(i * TILE, TILE)] = tile.T
 
-    def make_table():
-        @pl.loop(0, npr * CAP)
-        def _(q):
-            def pick(c, found):
-                return jnp.where(own_ref[0, c] == q, c, found)
-
-            table[q] = lax.fori_loop(0, npr, pick, jnp.int32(0))
-
     def grad_one(h, t):
         return remote(
             gs[h].at[t], g1[h].at[p],
@@ -246,18 +239,20 @@
 
     def finish_half(h):
         base = h * hrow
-        last = h * steps + steps - 1
-        for way in range(2):
-            rows = pl.ds(base + way * drow, drow)
-            part[way] = nn(ct[rows, :], a_all[z])
-            for sub in range(SUBS):
+        last = h * arc + arc - 1
+        part[0] = nn(ct[pl.ds(base, hrow), :], a_all[nz - 1])
+        for sub in range(SUBS):
+            for way in range(2):
                 ring(last, way, sub).wait_recv()
-                done = (
-                    part[way, pl.ds(sub * srow, srow), :] + rs_in[last, way, sub].astype(F32)
-                ).astype(BF)
-                gt[pl.ds(base + way * drow + sub * srow, srow), :] = done
-                first = (way * drow + sub * srow) // grow
-                gs[h][pl.ds(first, srow // grow)] = done.reshape(srow // grow, grow, blk)
+            done = (
+                part[0, pl.ds(sub * srow, srow), :]
+                + rs_in[last, 0, sub].astype(F32)
+                + rs_in[last, 1, sub].astype(F32)
+            ).astype(BF)
+            gt[pl.ds(base + sub * srow, srow), :] = done
+            gs[h][pl.ds(sub * srow // grow, srow // grow)] = done.reshape(
+                srow // grow, grow, blk
+            )
         peers(lambda t: grad_one(h, t).start())
 
     def turn_half(h):
@@ -271,68 +266,73 @@
 
         peers(lambda t: grad_two(h, t).start())
 
+    def rows_ready(k):
+        own_rows(k).wait()
+        twin_rows(k).wait_recv()
+
+    def far_end(way, sub):
+        return (way == 0) == (sub < SUBS // 2)
+
+    lanes = [(way, sub) for sub in range(SUBS) for way in range(2)]
+    lanes.sort(key=lambda lane: far_end(*lane))
+
+    def ring_step(h, s):
+        it = h * arc + s
+        mine = pl.ds(h * hrow, hrow)
+
+        @pl.when(s == 0)
+        def _():
+            part[0] = nn(ct[mine, :], a_all[0])
+
+        @pl.when(s > 0)
+        def _():
+            part[0] = nn(ct[mine, :], a_all[2 * s - 1])
+            part[1] = nn(ct[mine, :], a_all[2 * s])
+
+        for way, sub in lanes:
+            rows = pl.ds(sub * srow, srow)
+            begin = 0 if far_end(way, sub) else 1
+
+            @pl.when(s == begin)
+            def _():
+                rs_out[it, way, sub] = part[begin * way, rows, :].astype(BF)
+                ring(it, way, sub).start()
+
+            @pl.when(s > begin)
+            def _():
+                ring(it - 1, way, sub).wait_recv()
+                rs_out[it, way, sub] = (
+                    part[way, rows, :] + rs_in[it - 1, way, sub].astype(F32)
+                ).astype(BF)
+                ring(it, way, sub).start()
+
+    pack_stats()
     own_cot.wait()
     twin_cot.wait_recv()
     ct[...] = cbuf[...].T
 
-    @pl.loop(0, nz - 1)
-    def _(k):
-        own_rows(k).wait()
-        twin_rows(k).wait_recv()
-
-    own_rows(nz - 1).wait()
-    twin_rows(nz - 1).wait_recv()
-
-    @pl.loop(0, HALVES * steps)
-    def _(it):
-        h = it // steps
-        s = it % steps
-
-        for way in range(2):
-            dest = (z + nz - 1 - s) % nz if way == 0 else (z + 1 + s) % nz
-            rows = pl.ds(pl.multiple_of(h * hrow + way * drow, drow), drow)
-            part[way] = nn(ct[rows, :], a_all[dest])
-        for sub in range(SUBS):
-            for way in range(2):
-                rows = pl.ds(sub * srow, srow)
-
-                @pl.when(s == 0)
-                def _():
-                    rs_out[it, way, sub] = part[way, rows, :].astype(BF)
-
-                @pl.when(s > 0)
-                def _():
-                    ring(it - 1, way, sub).wait_recv()
-                    rs_out[it, way, sub] = (
-                        part[way, rows, :] + rs_in[it - 1, way, sub].astype(F32)
-                    ).astype(BF)
-
-                ring(it, way, sub).start()
-
-        @pl.when(it == 0)
+    @pl.loop(0, arc)
+    def _(s):
+        @pl.when(s > 0)
         def _():
-            pack_stats()
-
-        @pl.when(it == 1)
+            rows_ready(2 * s - 1)
+
+        rows_ready(2 * s)
+        for h in range(HALVES):
+            ring_step(h, s)
+
+        @pl.when(s == 0)
         def _():
-            make_table()
-
-        @pl.when(it == steps)
-        def _():
-            finish_half(0)
-
-        @pl.when(it == steps + 1)
+            peers(lambda t: stat_one(t).start())
+
+        @pl.when(s == arc - 2)
         def _():
             turn_stats()
 
-        @pl.when(it == steps + steps // 2)
-        def _():
-            turn_half(0)
-
-        @pl.when(it == 2 * steps - 1)
-        def _():
-            unpack_stats()
-
+    rows_ready(nz - 1)
+    finish_half(0)
+    unpack_stats()
+    turn_half(0)
     finish_half(1)
     g = gt[...]
     mats[1] += nt(g, g) * (1.0 / blk)
@@ -349,17 +349,20 @@
 
     twin_cot.wait_send()
 
-    @pl.loop(0, nz - 1)
+    @pl.loop(0, nz)
     def _(k):
         twin_rows(k).wait_send()
 
-    twin_rows(nz - 1).wait_send()
-
-    @pl.loop(0, HALVES * steps)
+    @pl.loop(0, HALVES * arc)
     def _(it):
-        for way in range(2):
-            for sub in range(SUBS):
+        for way, sub in lanes:
+            if far_end(way, sub):
                 ring(it, way, sub).wait_send()
+            else:
+
+                @pl.when(it % arc > 0)
+                def _():
+                    ring(it, way, sub).wait_send()
 
     def sent(t):
         stat_one(t).wait_send()
@@ -371,34 +374,61 @@
     peers(sent)
 
 
-def fresh_kernel(parts, own_ref, half_ref, xr_ref, slots_ref, left_ref, right_ref,
-                 upd_ref, lout_ref, rout_ref, g_scr):
-    step = pl.program_id(0)
-    slot = step // parts
-    piece = step % parts
-    blk = half_ref.shape[0]
-    rows = blk // parts
-    q = lax.axis_index("prec") * CAP + slot
-    named = jnp.int32(0)
-    for c in range(own_ref.shape[1]):
-        named = named + (own_ref[0, c] == q).astype(jnp.int32)
-
-    @pl.when(step == 0)
-    def _():
-        upd_ref[...] = nn(half_ref[...], xr_ref[...]).astype(BF)
-
-    @pl.when(named > 0)
-    def _():
-        at = pl.multiple_of(piece * rows, rows)
-        g = slots_ref[...].reshape(blk, blk)
-        g_scr[...] = g
-        lout_ref[0, 0] = DECAY * left_ref[0, 0] + tn(g_scr[:, pl.ds(at, rows)], g) * (1.0 / blk)
-        rout_ref[0, 0] = DECAY * right_ref[0, 0] + nt(g_scr[pl.ds(at, rows), :], g) * (1.0 / blk)
-
-    @pl.when(named == 0)
-    def _():
-        lout_ref[...] = left_ref[...]
-        rout_ref[...] = right_ref[...]
+def fresh_kernel(own_ref, half_ref, xr_ref, slots_ref, left_ref, right_ref,
+                 upd_ref, lout_ref, rout_ref, stat, g_scr, half, xr, upd, in_sem, out_sem):
+    blk = xr.shape[0]
+    first = lax.axis_index("prec") * CAP
+    stats_in, stats_out = (left_ref, right_ref), (lout_ref, rout_ref)
+    slabs = slots_ref.shape[1]
+    grow = slots_ref.shape[3]
+
+    def fetch(slot, m):
+        return pltpu.make_async_copy(
+            stats_in[m].at[0, slot], stat.at[slot, m], in_sem.at[slot * 2 + m]
+        )
+
+    def store(slot, m):
+        return pltpu.make_async_copy(
+            stat.at[slot, m], stats_out[m].at[0, slot], out_sem.at[slot * 2 + m]
+        )
+
+    def block(slot):
+        return pltpu.make_async_copy(
+            slots_ref.at[:, :, slot], g_scr.at[slot], in_sem.at[2 * CAP + slot]
+        )
+
+    half_in = pltpu.make_async_copy(half_ref, half, in_sem.at[3 * CAP])
+    xr_in = pltpu.make_async_copy(xr_ref, xr, in_sem.at[3 * CAP + 1])
+    upd_out = pltpu.make_async_copy(upd, upd_ref, out_sem.at[2 * CAP])
+
+    for slot in range(CAP):
+        block(slot).start()
+        fetch(slot, 0).start()
+        fetch(slot, 1).start()
+    half_in.start()
+    xr_in.start()
+    for slot in range(CAP):
+        named = jnp.int32(0)
+        for c in range(own_ref.shape[1]):
+            named = named + (own_ref[0, c] == first + slot).astype(jnp.int32)
+        block(slot).wait()
+        for m, product in ((1, nt), (0, tn)):
+            fetch(slot, m).wait()
+
+            @pl.when(named > 0)
+            def _():
+                g = g_scr[slot].reshape(HALVES * slabs * grow, blk)
+                stat[slot, m] = DECAY * stat[slot, m] + product(g, g) * (1.0 / blk)
+
+            store(slot, m).start()
+    half_in.wait()
+    xr_in.wait()
+    upd[...] = nn(half[...], xr[...]).astype(BF)
+    upd_out.start()
+    for slot in range(CAP):
+        for m in range(2):
+            store(slot, m).wait()
+    upd_out.wait()
 
 
 def shards(activations, cotangents, owner_slots, left_stats, right_stats):
@@ -406,9 +436,9 @@
     npr = lax.axis_size("prec")
     tok, blk = cotangents.shape
     nz = nd // 2
-    its = HALVES * (nz - 1)
+    its = HALVES * (nz // 2)
     hrow = blk // HALVES
-    srow = hrow // 2 // SUBS
+    srow = hrow // SUBS
     grow = hrow // npr
     srows = 2 * len(upper_tiles(blk)) * TILE // npr
     dma = pltpu.SemaphoreType.DMA
@@ -434,7 +464,7 @@
             pltpu.VMEM((npr, srows, TILE), BF),
             pltpu.VMEM((its, 2, SUBS, srow, blk), BF),
             pltpu.VMEM((its, 2, SUBS, srow, blk), BF),
-            pltpu.VMEM((2, hrow // 2, blk), F32),
+            pltpu.VMEM((2, hrow, blk), F32),
             pltpu.VMEM((blk, blk), BF),
             pltpu.VMEM((npr, grow, blk), BF),
             pltpu.VMEM((npr, grow, blk), BF),
@@ -469,28 +499,24 @@
         name="travel",
     )(owner_slots, activations, cotangents, left_stats, right_stats)
 
-    parts = 2
-    rows = blk // parts
-    stat_spec = pl.BlockSpec((1, 1, rows, blk), lambda i: (0, i // parts, i % parts, 0))
-    whole = pl.BlockSpec((blk, blk), lambda i: (0, 0))
     update, left_out, right_out = pl.pallas_call(
-        functools.partial(fresh_kernel, parts),
-        grid=(CAP * parts,),
+        fresh_kernel,
         out_shape=[
             jax.ShapeDtypeStruct((blk, blk), BF),
             jax.ShapeDtypeStruct(left_stats.shape, F32),
             jax.ShapeDtypeStruct(right_stats.shape, F32),
         ],
-        in_specs=[
-            pl.BlockSpec(memory_space=pltpu.SMEM),
-            whole,
-            whole,
-            pl.BlockSpec((HALVES, npr, 1, grow, blk), lambda i: (0, 0, i // parts, 0, 0)),
-            stat_spec,
-            stat_spec,
+        in_specs=[pl.BlockSpec(memory_space=pltpu.SMEM)] + [far] * 5,
+        out_specs=[far] * 3,
+        scratch_shapes=[
+            pltpu.VMEM((CAP, 2, blk, blk), F32),
+            pltpu.VMEM((CAP, HALVES, npr, grow, blk), BF),
+            pltpu.VMEM((blk, blk), BF),
+            pltpu.VMEM((blk, blk), BF),
+            pltpu.VMEM((blk, blk), BF),
+            dma((3 * CAP + 2,)),
+            dma((2 * CAP + 1,)),
         ],
-        out_specs=[whole, stat_spec, stat_spec],
-        scratch_shapes=[pltpu.VMEM((blk, blk), BF)],
         compiler_params=pltpu.CompilerParams(vmem_limit_bytes=60 * 1024 * 1024),
         name="fresh",
     )(owner_slots, half, xr, slots, left_stats, right_stats)

time: 97.8 us -> 87.7 us (0.90)
  Pallas kernels: 96.1 us -> 86.3 us
    pallas_call x1, Pallas kernels: 90.1 us -> 81.1 us  [shards(): pl.pallas_call(functools.partial(travel_kernel, nd, npr), out_shape=[jax....]
where the time goes in v2:
time: 87.7 us; the launch traced here: 87 us
  Pallas kernels  86.3 us (98%)
    pallas_call x1, Pallas kernels, shards(): pl.pallas_call(functools.partial(travel_kernel, nd, npr), out_shape=[jax....  81.1 us
    pallas_call x1, Pallas kernels, shards(): pl.pallas_call(fresh_kernel, out_shape=[jax.ShapeDtypeStruct((blk, blk),...  5.25 us

profile of v2, /device:TPU:24, one launch (start us, length us, event | category | flops | bytes accessed | tf_op | source)
XLA Modules:
  0.0 87.0 jit_solution(5519537496575960223)
XLA Ops:
  0.6 81.1 %travel.1 = (bf16[512,512]{1,0:T(8,128)(2,1)}, bf16[512,512]{1,0:T(8,128)(2,1)}, bf16[2,16,2,16,512]{4,3,2,1,0:T(8,128)(2,1)}) custom-call(s32[1,16]{1,0:T(1,128)} %own_ref.3, bf16[256,8192]{1,0:T(8,128)(2,1)} %act_ref.1, bf16[256,512]{1,0:T(8,128)(2,1)} %cot_ref.1, f32[1,2,512,512]{3,2,1,0:T(8,128)} %left_ref.3, f32[1,2,512,512]{3,2,1,0:T(8,128)} %right_ref.3), custom_call_target="tpu_custom_call" | custom-call | tf_op jit(solution)/shard_map/travel/pallas_call | solution.py:447
  81.7 5.2 %fresh.1 = (bf16[512,512]{1,0:T(8,128)(2,1)}, f32[1,2,512,512]{3,2,1,0:T(8,128)}, f32[1,2,512,512]{3,2,1,0:T(8,128)}) custom-call(s32[1,16]{1,0:T(1,128)} %own_ref.3, bf16[512,512]{1,0:T(8,128)(2,1)} %get-tuple-element.6.half_ref, bf16[512,512]{1,0:T(8,128)(2,1)} %get-tuple-element.7.xr_ref, bf16[2,16,2,16,512]{4,3,2,1,0:T(8,128)(2,1)} %get-tuple-element.8.slots_ref, ...), custom_call_target="tpu_custom_call" | custom-call | tf_op jit(solution)/shard_map/fresh/pallas_call | solution.py:502

commit v3 on v2

--- a/solution.py
+++ b/solution.py
@@ -311,29 +311,40 @@
     twin_cot.wait_recv()
     ct[...] = cbuf[...].T
 
-    @pl.loop(0, arc)
-    def _(s):
-        @pl.when(s > 0)
-        def _():
-            rows_ready(2 * s - 1)
-
-        rows_ready(2 * s)
-        for h in range(HALVES):
-            ring_step(h, s)
-
-        @pl.when(s == 0)
+    @pl.loop(0, arc + 2)
+    def _(j):
+        @pl.when((j > 0) & (j < arc))
+        def _():
+            rows_ready(2 * j - 1)
+
+        @pl.when(j < arc)
+        def _():
+            rows_ready(2 * j)
+            ring_step(0, j)
+
+        @pl.when(j == 0)
         def _():
             peers(lambda t: stat_one(t).start())
 
-        @pl.when(s == arc - 2)
+        @pl.when(j == arc)
+        def _():
+            rows_ready(nz - 1)
+            finish_half(0)
+
+        @pl.when(j >= 2)
+        def _():
+            ring_step(1, j - 2)
+
+        @pl.when(j == arc - 1)
         def _():
             turn_stats()
 
-    rows_ready(nz - 1)
-    finish_half(0)
+        @pl.when(j == arc + 1)
+        def _():
+            turn_half(0)
+
+    finish_half(1)
     unpack_stats()
-    turn_half(0)
-    finish_half(1)
     g = gt[...]
     mats[1] += nt(g, g) * (1.0 / blk)
     inverse_root(mats.at[1], xr_ref, f_scr)
@@ -375,60 +386,55 @@
 
 
 def fresh_kernel(own_ref, half_ref, xr_ref, slots_ref, left_ref, right_ref,
-                 upd_ref, lout_ref, rout_ref, stat, g_scr, half, xr, upd, in_sem, out_sem):
-    blk = xr.shape[0]
+                 upd_ref, lout_ref, rout_ref, stat, upd, out_sem):
+    blk = xr_ref.shape[0]
     first = lax.axis_index("prec") * CAP
     stats_in, stats_out = (left_ref, right_ref), (lout_ref, rout_ref)
-    slabs = slots_ref.shape[1]
-    grow = slots_ref.shape[3]
-
-    def fetch(slot, m):
+    quarter = blk // 2
+
+    def store(slot, m, part):
+        rows = pl.ds(part * quarter, quarter)
         return pltpu.make_async_copy(
-            stats_in[m].at[0, slot], stat.at[slot, m], in_sem.at[slot * 2 + m]
-        )
-
-    def store(slot, m):
-        return pltpu.make_async_copy(
-            stat.at[slot, m], stats_out[m].at[0, slot], out_sem.at[slot * 2 + m]
-        )
-
-    def block(slot):
-        return pltpu.make_async_copy(
-            slots_ref.at[:, :, slot], g_scr.at[slot], in_sem.at[2 * CAP + slot]
-        )
-
-    half_in = pltpu.make_async_copy(half_ref, half, in_sem.at[3 * CAP])
-    xr_in = pltpu.make_async_copy(xr_ref, xr, in_sem.at[3 * CAP + 1])
-    upd_out = pltpu.make_async_copy(upd, upd_ref, out_sem.at[2 * CAP])
-
-    for slot in range(CAP):
-        block(slot).start()
-        fetch(slot, 0).start()
-        fetch(slot, 1).start()
-    half_in.start()
-    xr_in.start()
+            stat.at[slot, m, rows], stats_out[m].at[0, slot, rows],
+            out_sem.at[(slot * 2 + m) * 2 + part],
+        )
+
+    upd_out = pltpu.make_async_copy(upd, upd_ref, out_sem.at[4 * CAP])
+    upd[...] = nn(half_ref[...], xr_ref[...]).astype(BF)
+    upd_out.start()
     for slot in range(CAP):
         named = jnp.int32(0)
         for c in range(own_ref.shape[1]):
             named = named + (own_ref[0, c] == first + slot).astype(jnp.int32)
-        block(slot).wait()
-        for m, product in ((1, nt), (0, tn)):
-            fetch(slot, m).wait()
-
-            @pl.when(named > 0)
-            def _():
-                g = g_scr[slot].reshape(HALVES * slabs * grow, blk)
-                stat[slot, m] = DECAY * stat[slot, m] + product(g, g) * (1.0 / blk)
-
-            store(slot, m).start()
-    half_in.wait()
-    xr_in.wait()
-    upd[...] = nn(half[...], xr[...]).astype(BF)
-    upd_out.start()
+
+        @pl.when(named > 0)
+        def _():
+            g = slots_ref[:, :, slot].reshape(blk, blk)
+            for m, product in ((1, nt), (0, tn)):
+                for part in range(2):
+                    rows = slice(part * quarter, (part + 1) * quarter)
+                    piece = g[rows, :] if m else g[:, rows]
+                    stat[slot, m, rows] = DECAY * stats_in[m][0, slot, rows] + product(
+                        piece, g
+                    ) * (1.0 / blk)
+                    store(slot, m, part).start()
+
+        @pl.when(named == 0)
+        def _():
+            for m in range(2):
+                stat[slot, m] = stats_in[m][0, slot]
+                for part in range(2):
+                    store(slot, m, part).start()
+
+    upd_out.wait()
     for slot in range(CAP):
         for m in range(2):
-            store(slot, m).wait()
-    upd_out.wait()
+            for part in range(2):
+                store(slot, m, part).wait()
+
+
+def in_hbm(array):
+    return pltpu.with_memory_space_constraint(array, pltpu.HBM)
 
 
 def shards(activations, cotangents, owner_slots, left_stats, right_stats):
@@ -494,10 +500,10 @@
             dma((HALVES, npr)),
         ],
         compiler_params=pltpu.CompilerParams(
-            collective_id=0, has_side_effects=True, vmem_limit_bytes=60 * 1024 * 1024
+            collective_id=0, has_side_effects=True, vmem_limit_bytes=44 * 1024 * 1024
         ),
         name="travel",
-    )(owner_slots, activations, cotangents, left_stats, right_stats)
+    )(*[in_hbm(a) for a in (owner_slots, activations, cotangents, left_stats, right_stats)])
 
     update, left_out, right_out = pl.pallas_call(
         fresh_kernel,
@@ -506,18 +512,14 @@
             jax.ShapeDtypeStruct(left_stats.shape, F32),
             jax.ShapeDtypeStruct(right_stats.shape, F32),
         ],
-        in_specs=[pl.BlockSpec(memory_space=pltpu.SMEM)] + [far] * 5,
+        in_specs=[pl.BlockSpec(memory_space=pltpu.SMEM)] + [vmem] * 5,
         out_specs=[far] * 3,
         scratch_shapes=[
             pltpu.VMEM((CAP, 2, blk, blk), F32),
-            pltpu.VMEM((CAP, HALVES, npr, grow, blk), BF),
             pltpu.VMEM((blk, blk), BF),
-            pltpu.VMEM((blk, blk), BF),
-            pltpu.VMEM((blk, blk), BF),
-            dma((3 * CAP + 2,)),
-            dma((2 * CAP + 1,)),
+            dma((4 * CAP + 1,)),
         ],
-        compiler_params=pltpu.CompilerParams(vmem_limit_bytes=60 * 1024 * 1024),
+        compiler_params=pltpu.CompilerParams(vmem_limit_bytes=32 * 1024 * 1024),
         name="fresh",
     )(owner_slots, half, xr, slots, left_stats, right_stats)
     return (update, left_out, right_out)

time: 87.7 us -> 78.4 us (0.89)
  Pallas kernels: 86.3 us -> 77.6 us
    pallas_call x1, Pallas kernels: 81.1 us -> 74.1 us  [shards(): pl.pallas_call(functools.partial(travel_kernel, nd, npr), out_shape=[jax....]
    pallas_call x1, Pallas kernels: 5.25 us -> 3.51 us  [shards(): pl.pallas_call(fresh_kernel, out_shape=[jax.ShapeDtypeStruct((blk, blk),...]
where the time goes in v3:
time: 78.4 us; the launch traced here: 78.3 us
  Pallas kernels  77.6 us (99%)
    pallas_call x1, Pallas kernels, shards(): pl.pallas_call(functools.partial(travel_kernel, nd, npr), out_shape=[jax....  74.1 us
    pallas_call x1, Pallas kernels, shards(): pl.pallas_call(fresh_kernel, out_shape=[jax.ShapeDtypeStruct((blk, blk),...  3.51 us

profile of v3, /device:TPU:24, one launch (start us, length us, event | category | flops | bytes accessed | tf_op | source)
XLA Modules:
  0.0 78.3 jit_solution(2585306976162058286)
XLA Ops:
  0.6 0.0 copy-start.1
  0.6 0.0 copy-start
  0.7 0.0 copy-start.2
  0.7 74.1 %travel.1 = (bf16[512,512]{1,0:T(8,128)(2,1)S(1)}, bf16[512,512]{1,0:T(8,128)(2,1)S(1)}, bf16[2,16,2,16,512]{4,3,2,1,0:T(8,128)(2,1)S(1)}) custom-call(s32[1,16]{1,0:T(1,128)} %own_ref.3, bf16[256,8192]{1,0:T(8,128)(2,1)} %act_ref.1, bf16[256,512]{1,0:T(8,128)(2,1)} %cot_ref.1, f32[1,2,512,512]{3,2,1,0:T(8,128)} %left_ref.3, f32[1,2,512,512]{3,2,1,0:T(8,128)} %right_ref.3), custom_call_target="tpu_custom_call" | custom-call | tf_op jit(solution)/shard_map/travel/pallas_call | solution.py:453
  74.8 0.0 copy-done.1
  74.8 0.0 copy-done
  74.8 0.0 copy-done.2
  74.8 3.5 %fresh.1 = (bf16[512,512]{1,0:T(8,128)(2,1)}, f32[1,2,512,512]{3,2,1,0:T(8,128)}, f32[1,2,512,512]{3,2,1,0:T(8,128)}) custom-call(s32[1,16]{1,0:T(1,128)S(1)} %copy-done.2, bf16[512,512]{1,0:T(8,128)(2,1)S(1)} %get-tuple-element.6.half_ref, bf16[512,512]{1,0:T(8,128)(2,1)S(1)} %get-tuple-element.7.xr_ref, ...), custom_call_target="tpu_custom_call" | custom-call | tf_op jit(solution)/shard_map/fresh/pallas_call | solution.py:508
Async XLA Ops:
  0.6 74.2 %copy-start.1 = (f32[1,2,512,512]{3,2,1,0:T(8,128)S(1)}, f32[1,2,512,512]{3,2,1,0:T(8,128)}, u32[]{:S(2)}) copy-start(f32[1,2,512,512]{3,2,1,0:T(8,128)} %right_ref.3) | copy-start | bytes 6291460
  0.6 74.2 %copy-start = (f32[1,2,512,512]{3,2,1,0:T(8,128)S(1)}, f32[1,2,512,512]{3,2,1,0:T(8,128)}, u32[]{:S(2)}) copy-start(f32[1,2,512,512]{3,2,1,0:T(8,128)} %left_ref.3) | copy-start | bytes 6291460
  0.7 74.2 %copy-start.2 = (s32[1,16]{1,0:T(1,128)S(1)}, s32[1,16]{1,0:T(1,128)}, u32[]{:S(2)}) copy-start(s32[1,16]{1,0:T(1,128)} %own_ref.3) | copy-start | bytes 196

commit v4 on v3

--- a/solution.py
+++ b/solution.py
@@ -62,8 +62,8 @@
 def travel_kernel(
     nd, npr,
     own_ref, act_ref, cot_ref, left_ref, right_ref,
-    half_ref, xr_ref, slots_ref,
-    a_all, cbuf, ct, stat, pk1, st1, pk2, st2, rs_out, rs_in, part, gt, gsa, gsb, g1a, g1b, pk3a, pk3b, sla, slb, mats, f_scr, xl,
+    upd_ref, slots_ref,
+    a_all, cbuf, ct, cx, stat, pk1, st1, pk2, st2, rs_out, rs_in, part, gt, gsa, gsb, g1a, g1b, pk3a, pk3b, sla, slb, mats, f_scr, xl, xr_ref,
     table,
     loc_sem, stat_sem, xs, xr, rss, rsr, s1s, s1r, s2s, s2r, g1s, g1r, g2s, g2r,
 ):
@@ -115,8 +115,8 @@
             act_ref.at[:, cols], a_all.at[k, pl.ds(tok, tok)], xs.at[k], xr.at[k], dp=twin
         )
 
-    own_cot = pltpu.make_async_copy(cot_ref, cbuf.at[pl.ds(0, tok)], loc_sem.at[nz])
-    twin_cot = remote(cot_ref, cbuf.at[pl.ds(tok, tok)], xs.at[nz], xr.at[nz], dp=twin)
+    own_cot = pltpu.make_async_copy(cot_ref, cbuf, loc_sem.at[nz])
+    twin_cot = remote(ct, cx, xs.at[nz], xr.at[nz], dp=twin)
     left_in = pltpu.make_async_copy(left_ref.at[0], stat.at[0], stat_sem.at[0])
     right_in = pltpu.make_async_copy(right_ref.at[0], stat.at[1], stat_sem.at[1])
 
@@ -143,6 +143,8 @@
     peers(
         lambda t: pl.semaphore_signal(barrier, inc=1, device_id={"prec": t}, device_id_type=MESH)
     )
+    own_cot.wait()
+    ct[...] = cbuf[...].T
     make_table()
     pl.semaphore_wait(barrier, 3 + npr - 1)
 
@@ -237,10 +239,13 @@
             dp=up if way == 0 else down,
         )
 
+    def product(rows, k):
+        return nn(ct[rows, :], a_all[k, pl.ds(0, tok)]) + nn(cx[rows, :], a_all[k, pl.ds(tok, tok)])
+
     def finish_half(h):
         base = h * hrow
         last = h * arc + arc - 1
-        part[0] = nn(ct[pl.ds(base, hrow), :], a_all[nz - 1])
+        part[0] = product(pl.ds(base, hrow), nz - 1)
         for sub in range(SUBS):
             for way in range(2):
                 ring(last, way, sub).wait_recv()
@@ -282,12 +287,12 @@
 
         @pl.when(s == 0)
         def _():
-            part[0] = nn(ct[mine, :], a_all[0])
+            part[0] = product(mine, 0)
 
         @pl.when(s > 0)
         def _():
-            part[0] = nn(ct[mine, :], a_all[2 * s - 1])
-            part[1] = nn(ct[mine, :], a_all[2 * s])
+            part[0] = product(mine, 2 * s - 1)
+            part[1] = product(mine, 2 * s)
 
         for way, sub in lanes:
             rows = pl.ds(sub * srow, srow)
@@ -307,11 +312,10 @@
                 ring(it, way, sub).start()
 
     pack_stats()
-    own_cot.wait()
+    peers(lambda t: stat_one(t).start())
     twin_cot.wait_recv()
-    ct[...] = cbuf[...].T
-
-    @pl.loop(0, arc + 2)
+
+    @pl.loop(0, arc + 3)
     def _(j):
         @pl.when((j > 0) & (j < arc))
         def _():
@@ -322,24 +326,20 @@
             rows_ready(2 * j)
             ring_step(0, j)
 
-        @pl.when(j == 0)
-        def _():
-            peers(lambda t: stat_one(t).start())
-
         @pl.when(j == arc)
         def _():
             rows_ready(nz - 1)
             finish_half(0)
 
-        @pl.when(j >= 2)
-        def _():
-            ring_step(1, j - 2)
+        @pl.when(j >= 3)
+        def _():
+            ring_step(1, j - 3)
 
         @pl.when(j == arc - 1)
         def _():
             turn_stats()
 
-        @pl.when(j == arc + 1)
+        @pl.when(j == arc + 2)
         def _():
             turn_half(0)
 
@@ -351,7 +351,8 @@
     turn_half(1)
     mats[0] += tn(g, g) * (1.0 / blk)
     inverse_root(mats.at[0], xl, f_scr)
-    half_ref[...] = nt(xl[...], gt[...]).astype(BF)
+    half = nt(xl[...], gt[...]).astype(BF)
+    upd_ref[...] = nn(half, xr_ref[...]).astype(BF)
 
     for h in range(HALVES):
         peers(lambda u, h=h: grad_two_from(h, u).wait_recv())
@@ -385,9 +386,9 @@
     peers(sent)
 
 
-def fresh_kernel(own_ref, half_ref, xr_ref, slots_ref, left_ref, right_ref,
-                 upd_ref, lout_ref, rout_ref, stat, upd, out_sem):
-    blk = xr_ref.shape[0]
+def fresh_kernel(own_ref, prepared_ref, slots_ref, left_ref, right_ref,
+                 upd_ref, lout_ref, rout_ref, stat, out_sem):
+    blk = prepared_ref.shape[0]
     first = lax.axis_index("prec") * CAP
     stats_in, stats_out = (left_ref, right_ref), (lout_ref, rout_ref)
     quarter = blk // 2
@@ -399,8 +400,7 @@
             out_sem.at[(slot * 2 + m) * 2 + part],
         )
 
-    upd_out = pltpu.make_async_copy(upd, upd_ref, out_sem.at[4 * CAP])
-    upd[...] = nn(half_ref[...], xr_ref[...]).astype(BF)
+    upd_out = pltpu.make_async_copy(prepared_ref, upd_ref, out_sem.at[4 * CAP])
     upd_out.start()
     for slot in range(CAP):
         named = jnp.int32(0)
@@ -450,19 +450,19 @@
     dma = pltpu.SemaphoreType.DMA
     vmem = pl.BlockSpec(memory_space=pltpu.VMEM)
     far = pl.BlockSpec(memory_space=pltpu.HBM)
-    half, xr, slots = pl.pallas_call(
+    prepared, slots = pl.pallas_call(
         functools.partial(travel_kernel, nd, npr),
         out_shape=[
-            jax.ShapeDtypeStruct((blk, blk), BF),
             jax.ShapeDtypeStruct((blk, blk), BF),
             jax.ShapeDtypeStruct((HALVES, npr, CAP, grow, blk), BF),
         ],
         in_specs=[pl.BlockSpec(memory_space=pltpu.SMEM)] + [far] * 4,
-        out_specs=[vmem] * 3,
+        out_specs=[vmem] * 2,
         scratch_shapes=[
             pltpu.VMEM((nz, 2 * tok, blk), BF),
-            pltpu.VMEM((2 * tok, blk), BF),
-            pltpu.VMEM((blk, 2 * tok), BF),
+            pltpu.VMEM((tok, blk), BF),
+            pltpu.VMEM((blk, tok), BF),
+            pltpu.VMEM((blk, tok), BF),
             pltpu.VMEM((2, CAP, blk, blk), F32),
             pltpu.VMEM((npr, CAP, srows, TILE), BF),
             pltpu.VMEM((npr * CAP, srows, TILE), BF),
@@ -482,6 +482,7 @@
             pltpu.VMEM((npr, CAP, grow, blk), BF),
             pltpu.VMEM((2, blk, blk), F32),
             pltpu.VMEM((blk, blk), F32),
+            pltpu.VMEM((blk, blk), BF),
             pltpu.VMEM((blk, blk), BF),
             pltpu.SMEM((npr * CAP,), jnp.int32),
             dma((nz + 1,)),
@@ -512,16 +513,15 @@
             jax.ShapeDtypeStruct(left_stats.shape, F32),
             jax.ShapeDtypeStruct(right_stats.shape, F32),
         ],
-        in_specs=[pl.BlockSpec(memory_space=pltpu.SMEM)] + [vmem] * 5,
+        in_specs=[pl.BlockSpec(memory_space=pltpu.SMEM)] + [vmem] * 4,
         out_specs=[far] * 3,
         scratch_shapes=[
             pltpu.VMEM((CAP, 2, blk, blk), F32),
-            pltpu.VMEM((blk, blk), BF),
             dma((4 * CAP + 1,)),
         ],
         compiler_params=pltpu.CompilerParams(vmem_limit_bytes=32 * 1024 * 1024),
         name="fresh",
-    )(owner_slots, half, xr, slots, left_stats, right_stats)
+    )(owner_slots, prepared, slots, left_stats, right_stats)
     return (update, left_out, right_out)
 
 

time: 78.4 us -> 77.7 us (level)
  no operation moved by 1% of the time
where the time goes in v4:
time: 77.7 us; the launch traced here: 77.6 us
  Pallas kernels  76.9 us (99%)
    pallas_call x1, Pallas kernels, shards(): pl.pallas_call(functools.partial(travel_kernel, nd, npr), out_shape=[jax....  73.8 us
    pallas_call x1, Pallas kernels, shards(): pl.pallas_call(fresh_kernel, out_shape=[jax.ShapeDtypeStruct((blk, blk),...  3.09 us

profile of v4, /device:TPU:24, one launch (start us, length us, event | category | flops | bytes accessed | tf_op | source)
XLA Modules:
  0.0 77.6 jit_solution(5910531533163010215)
XLA Ops:
  0.6 0.0 copy-start.1
  0.6 0.0 copy-start
  0.7 0.0 copy-start.2
  0.7 73.8 %travel.1 = (bf16[512,512]{1,0:T(8,128)(2,1)S(1)}, bf16[2,16,2,16,512]{4,3,2,1,0:T(8,128)(2,1)S(1)}) custom-call(s32[1,16]{1,0:T(1,128)} %own_ref.3, bf16[256,8192]{1,0:T(8,128)(2,1)} %act_ref.1, bf16[256,512]{1,0:T(8,128)(2,1)} %cot_ref.1, f32[1,2,512,512]{3,2,1,0:T(8,128)} %left_ref.3, f32[1,2,512,512]{3,2,1,0:T(8,128)} %right_ref.3), custom_call_target="tpu_custom_call" | custom-call | tf_op jit(solution)/shard_map/travel/pallas_call | solution.py:453
  74.5 0.0 copy-done.1
  74.5 0.0 copy-done
  74.5 0.0 copy-done.2
  74.5 3.1 %fresh.1 = (bf16[512,512]{1,0:T(8,128)(2,1)}, f32[1,2,512,512]{3,2,1,0:T(8,128)}, f32[1,2,512,512]{3,2,1,0:T(8,128)}) custom-call(s32[1,16]{1,0:T(1,128)S(1)} %copy-done.2, bf16[512,512]{1,0:T(8,128)(2,1)S(1)} %get-tuple-element.5.prepared_ref, bf16[2,16,2,16,512]{4,3,2,1,0:T(8,128)(2,1)S(1)} %get-tuple-element.6.slots_ref, f32[1,2,512,512]{3,2,1,0:T(8,128)S(1)} %copy-done, ...), custom_call_target="tpu_custom_call" | custom-call | tf_op jit(solution)/shard_map/fresh/pallas_call | solution.py:509
Async XLA Ops:
  0.6 73.8 %copy-start.1 = (f32[1,2,512,512]{3,2,1,0:T(8,128)S(1)}, f32[1,2,512,512]{3,2,1,0:T(8,128)}, u32[]{:S(2)}) copy-start(f32[1,2,512,512]{3,2,1,0:T(8,128)} %right_ref.3) | copy-start | bytes 6291460
  0.6 73.8 %copy-start = (f32[1,2,512,512]{3,2,1,0:T(8,128)S(1)}, f32[1,2,512,512]{3,2,1,0:T(8,128)}, u32[]{:S(2)}) copy-start(f32[1,2,512,512]{3,2,1,0:T(8,128)} %left_ref.3) | copy-start | bytes 6291460
  0.7 73.8 %copy-start.2 = (s32[1,16]{1,0:T(1,128)S(1)}, s32[1,16]{1,0:T(1,128)}, u32[]{:S(2)}) copy-start(s32[1,16]{1,0:T(1,128)} %own_ref.3) | copy-start | bytes 196

commit v5 on v4

--- a/solution.py
+++ b/solution.py
@@ -339,7 +339,7 @@
         def _():
             turn_stats()
 
-        @pl.when(j == arc + 2)
+        @pl.when(j == arc + 1)
         def _():
             turn_half(0)
 

time: 77.7 us -> 77 us (level)
  Pallas kernels: 76.9 us -> 76 us
where the time goes in v5:
time: 77 us; the launch traced here: 76.7 us
  Pallas kernels  76 us (99%)
    pallas_call x1, Pallas kernels, shards(): pl.pallas_call(functools.partial(travel_kernel, nd, npr), out_shape=[jax....  73.2 us
    pallas_call x1, Pallas kernels, shards(): pl.pallas_call(fresh_kernel, out_shape=[jax.ShapeDtypeStruct((blk, blk),...  2.79 us

profile of v5, /device:TPU:24, one launch (start us, length us, event | category | flops | bytes accessed | tf_op | source)
XLA Modules:
  0.0 76.7 jit_solution(16923593693754871895)
XLA Ops:
  0.6 0.0 copy-start.1
  0.6 0.0 copy-start
  0.7 0.0 copy-start.2
  0.7 73.2 %travel.1 = (bf16[512,512]{1,0:T(8,128)(2,1)S(1)}, bf16[2,16,2,16,512]{4,3,2,1,0:T(8,128)(2,1)S(1)}) custom-call(s32[1,16]{1,0:T(1,128)} %own_ref.3, bf16[256,8192]{1,0:T(8,128)(2,1)} %act_ref.1, bf16[256,512]{1,0:T(8,128)(2,1)} %cot_ref.1, f32[1,2,512,512]{3,2,1,0:T(8,128)} %left_ref.3, f32[1,2,512,512]{3,2,1,0:T(8,128)} %right_ref.3), custom_call_target="tpu_custom_call" | custom-call | tf_op jit(solution)/shard_map/travel/pallas_call | solution.py:453
  73.9 0.0 copy-done.1
  73.9 0.0 copy-done
  73.9 0.0 copy-done.2
  73.9 2.8 %fresh.1 = (bf16[512,512]{1,0:T(8,128)(2,1)}, f32[1,2,512,512]{3,2,1,0:T(8,128)}, f32[1,2,512,512]{3,2,1,0:T(8,128)}) custom-call(s32[1,16]{1,0:T(1,128)S(1)} %copy-done.2, bf16[512,512]{1,0:T(8,128)(2,1)S(1)} %get-tuple-element.5.prepared_ref, bf16[2,16,2,16,512]{4,3,2,1,0:T(8,128)(2,1)S(1)} %get-tuple-element.6.slots_ref, f32[1,2,512,512]{3,2,1,0:T(8,128)S(1)} %copy-done, ...), custom_call_target="tpu_custom_call" | custom-call | tf_op jit(solution)/shard_map/fresh/pallas_call | solution.py:509
Async XLA Ops:
  0.6 73.3 %copy-start.1 = (f32[1,2,512,512]{3,2,1,0:T(8,128)S(1)}, f32[1,2,512,512]{3,2,1,0:T(8,128)}, u32[]{:S(2)}) copy-start(f32[1,2,512,512]{3,2,1,0:T(8,128)} %right_ref.3) | copy-start | bytes 6291460
  0.6 73.3 %copy-start = (f32[1,2,512,512]{3,2,1,0:T(8,128)S(1)}, f32[1,2,512,512]{3,2,1,0:T(8,128)}, u32[]{:S(2)}) copy-start(f32[1,2,512,512]{3,2,1,0:T(8,128)} %left_ref.3) | copy-start | bytes 6291460
  0.7 73.3 %copy-start.2 = (s32[1,16]{1,0:T(1,128)S(1)}, s32[1,16]{1,0:T(1,128)}, u32[]{:S(2)}) copy-start(s32[1,16]{1,0:T(1,128)} %own_ref.3) | copy-start | bytes 196
